TPU v7x, 32 devices: a whole 2x2x4 slice. The times are simulated.
32 devices in a mesh: band: 2 (over x), tm: 16 (over z, y, core).
Axes of the slice: x: 2, y: 2, z: 4, core: 2. Of those that a mesh axis runs over, the one named last changes fastest.
Arguments:
- voltages: bfloat16 [65536, 2048], P(('band', 'tm')), parts along dimension 0, may hold values from -6 to 6
- panel_map: int32 [2048], replicated, may hold values from 0 to 2047, each once
- block_list: int32 [16, 2], replicated, may hold values from 0 to 15, as said below
Outputs:
- visibilities: float32 [32, 2, 256, 128, 128], P('band', None, 'tm'), parts along dimension 0
There are 2 independent parts, one for each index of `band`. A program takes and returns all parts, laid end to end along the dimension named above; an argument that names none is the same for every part. Nothing has to cross between parts.
Inputs may be any that keep to these rules, and one draw needn't show every extreme that they name: `block_list`: each row is a pair of panel numbers; the list names exactly 8 distinct panels, among them panel 0 and panel 16 - 1, every one of them in its first column.
All inputs are finite; a program needn't handle non-finite values.
Results may differ from a plain program's by a relative error of at most 0.0064.
Values may be sent and summed in bfloat16 or wider, within the bound.
A program may use at most 128 MiB of HBM per device.

v0:
```python
import jax
import jax.numpy as jnp
from jax import lax
from jax.sharding import PartitionSpec as P

CHANNELS = 256
TAPS = 4
PANEL = 128


def from_behind(block, axis, distance):
    devices = range(lax.axis_size(axis))
    route = [(i - distance, i) for i in devices if i - distance in devices]
    return lax.ppermute(block, axis, route)


def filter_taps(taps, frame):
    length = taps * frame
    place = jnp.arange(length).astype(jnp.float32)
    middle = (length - 1) / 2.0
    window = 0.5 - 0.5 * jnp.cos(2.0 * jnp.pi * (place + 0.5) / length)
    shape_h = jnp.sinc((place - middle) / frame) * window
    shape_h = shape_h / jnp.sqrt(jnp.sum(shape_h * shape_h))
    return shape_h.reshape(taps, frame).astype(jnp.float32)


def dft_table(channels):
    frame = 2 * channels
    rows_k = jnp.arange(channels, dtype=jnp.int32)[:, None]
    cols_n = jnp.arange(frame, dtype=jnp.int32)[None, :]
    phase = (rows_k * cols_n % frame).astype(jnp.float32) * (2.0 * jnp.pi / frame)
    return jnp.concatenate([jnp.cos(phase), -jnp.sin(phase)], axis=0).astype(jnp.bfloat16)


def body(voltages, panel_map, block_list):
    frame = 2 * CHANNELS
    spec_dev = voltages.shape[0] // frame
    groups = lax.axis_size("tm")
    band_dev = CHANNELS // groups
    panel_rows = panel_map.reshape(-1, PANEL)
    columns = panel_rows[block_list]
    width = voltages.shape[1]
    frames = voltages.reshape(spec_dev, frame, width)
    earlier = from_behind(frames[spec_dev - (TAPS - 1) :], "tm", 1)
    padded = jnp.concatenate([earlier, frames], axis=0)
    coeff = filter_taps(TAPS, frame)
    filtered = jnp.zeros((spec_dev, frame, width), jnp.float32)
    for tap in range(TAPS):
        filtered = filtered + coeff[tap][None, :, None] * padded[tap : tap + spec_dev].astype(
            jnp.float32
        )
    filtered = filtered.astype(jnp.bfloat16)
    table = dft_table(CHANNELS)
    spectra = jnp.einsum("kn,sni->ski", table, filtered, preferred_element_type=jnp.float32)
    spectra = spectra.astype(jnp.bfloat16).reshape(spec_dev, 2, groups, band_dev, width)
    data = lax.all_to_all(spectra, "tm", split_axis=2, concat_axis=0, tiled=True)[:, :, 0]
    total = data.shape[0]
    first = data[:, :, :, columns[:, 0]]
    second = data[:, :, :, columns[:, 1]]
    flipped = jnp.stack([first[:, 1], -first[:, 0]], axis=1)
    real_part = jnp.einsum("sckbi,sckbj->bkij", first, second, preferred_element_type=jnp.float32)
    imag_part = jnp.einsum("sckbi,sckbj->bkij", flipped, second, preferred_element_type=jnp.float32)
    return jnp.stack([real_part, imag_part], axis=1) / total


def solution(mesh):
    in_specs = (P(("band", "tm"), None), P(), P())
    out_specs = P("band", None, "tm", None, None)
    return jax.shard_map(body, mesh=mesh, in_specs=in_specs, out_specs=out_specs, check_vma=False)
```

profile of v0, /device:TPU:13, one launch (start us, length us, event | category | flops | bytes accessed | tf_op | source)
XLA Modules:
  0.0 472.7 jit_solution(12410593673535821267)
XLA Ops:
  0.0 0.0 copy-start
  0.0 6.6 %slice.44 = bf16[1536,2048]{1,0:T(8,128)(2,1)} slice(bf16[2048,2048]{1,0:T(8,128)(2,1)} %param.3), slice={[512:2048], [0:2048]} | slice | bytes 12582912 | tf_op jit(solution)/shard_map/slice | solution.py:44
  6.6 3.7 collective-permute-start
  10.3 0.6 multiply_reduce_fusion
  11.6 0.1 broadcast_divide_fusion
  11.6 2.2 negate_convert_fusion
  13.8 64.7 %collective-permute-done = bf16[3,512,2048]{2,1,0:T(8,128)(2,1)} collective-permute-done((bf16[3,512,2048]{2,1,0:T(8,128)(2,1)}, bf16[3,512,2048]{2,1,0:T(8,128)(2,1)}, u32[]{:S(2)}, u32[]{:S(2)}) %collective-permute-start) | collective-permute-done | bytes 6291488 | tf_op jit(solution)/shard_map/ppermute | solution.py:14
  78.5 17.1 %fusion.6 = bf16[4,2048,512]{1,2,0:T(8,128)(2,1)} fusion(bf16[4,512,2048]{2,1,0:T(8,128)(2,1)} %bitcast.51, bf16[3,512,2048]{2,1,0:T(8,128)(2,1)} %collective-permute-done, f32[512]{0:T(512)S(1)} %get-tuple-element.10, f32[512]{0:T(512)S(1)} %get-tuple-element.11, f32[512]{0:T(512)S(1)} %get-tuple-element.12, f32[512]{0:T(512)S(1)} %get-tuple-element.9, ...), kind=kOutput, calls=%fused_computation.18 | convolution fusion | flops 4388290560 | bytes 23601152 | tf_op jit(solution)/shard_map/kn,sni->ski/dot_general | solution.py:54
  95.6 0.0 copy-start.2
  95.6 8.3 %copy.7 = bf16[4,2,16,16,2048]{4,3,1,0,2:T(8,128)(2,1)} copy(bf16[4,2,16,16,2048]{4,3,2,1,0:T(8,128)(2,1)} %bitcast.50) | data formatting | bytes 16777216 | tf_op jit(solution)/shard_map/reshape | solution.py:55
  103.9 7.2 %all-to-all-start = ((bf16[4,2,16,16,2048]{4,3,1,0,2:T(8,128)(2,1)}), bf16[4,2,16,16,2048]{4,3,1,0,2:T(8,128)(2,1)}, u32[]{:S(2)}, u32[]{:S(2)}) async-start(bf16[4,2,16,16,2048]{4,3,1,0,2:T(8,128)(2,1)} %copy.7), calls=%async_computation | async-start | bytes 16777216 | tf_op jit(solution)/shard_map/all_to_all | solution.py:56
  111.1 0.0 copy-done.2
  111.1 0.1 copy.8
  111.2 0.1 reshape.85
  111.3 0.0 copy-done
  111.3 0.6 gather_fusion
  112.0 181.5 %all-to-all-done = bf16[4,2,16,16,2048]{4,3,1,0,2:T(8,128)(2,1)} async-done(((bf16[4,2,16,16,2048]{4,3,1,0,2:T(8,128)(2,1)}), bf16[4,2,16,16,2048]{4,3,1,0,2:T(8,128)(2,1)}, u32[]{:S(2)}, u32[]{:S(2)}) %all-to-all-start) | async-done | bytes 8388640 | tf_op jit(solution)/shard_map/all_to_all | solution.py:56
  293.5 26.8 %copy.9 = bf16[64,2,16,2048]{0,2,3,1:T(8,128)(2,1)} copy(bf16[64,2,16,2048]{3,2,1,0:T(8,128)(2,1)} %bitcast.7) | data formatting | bytes 16777216 | tf_op jit(solution)/shard_map/squeeze | solution.py:56
  320.3 25.9 %gather_fusion.2 = bf16[2048,64,2,16]{1,3,2,0:T(8,128)(2,1)} fusion(bf16[64,2,16,2048]{0,2,3,1:T(8,128)(2,1)} %copy.9, s32[2048]{0:T(1024)S(1)} %fusion.26), kind=kCustom, calls=%fused_computation.2 | custom fusion | bytes 16785408 | tf_op jit(solution)/shard_map/gather | solution.py:59
  346.2 25.9 %gather_fusion.1 = bf16[2048,64,2,16]{1,3,2,0:T(8,128)(2,1)} fusion(bf16[64,2,16,2048]{0,2,3,1:T(8,128)(2,1)} %copy.9, s32[2048]{0:T(1024)S(1)} %fusion.24), kind=kCustom, calls=%fused_computation.1 | custom fusion | bytes 16785408 | tf_op jit(solution)/shard_map/gather | solution.py:58
  372.0 21.0 %copy.11 = bf16[16,128,64,2,16]{1,2,3,4,0:T(8,128)(2,1)} copy(bf16[16,128,64,2,16]{2,4,3,1,0:T(8,128)(2,1)} %bitcast.49) | data formatting | bytes 16777216 | tf_op jit(solution)/shard_map/gather | solution.py:58
  393.1 21.1 %copy.15 = bf16[64,2,16,16,128]{4,0,1,2,3:T(8,128)(2,1)} copy(bf16[64,2,16,16,128]{0,2,1,4,3:T(8,128)(2,1)} %bitcast.48) | data formatting | bytes 16777216 | tf_op jit(solution)/shard_map/gather | solution.py:59
  414.1 5.8 %fusion.35 = (bf16[64,1,16,16,128]{4,0,1,2,3:T(8,128)(2,1)}, bf16[64,1,16,16,128]{4,0,1,2,3:T(8,128)(2,1)}) fusion(bf16[64,2,16,16,128]{4,0,1,2,3:T(8,128)(2,1)} %bitcast.47), kind=kLoop, calls=%fused_computation.71 | loop fusion | flops 2097152 | bytes 16777216 | tf_op jit(solution)/shard_map/slice | solution.py:60
  420.0 14.4 %convolution_bitcast_fusion.1 = f32[16,1,16,128,128]{4,3,2,0,1:T(8,128)} fusion(bf16[64,2,16,16,128]{4,0,1,2,3:T(8,128)(2,1)} %copy.15, bf16[16,128,64,2,16]{1,2,3,4,0:T(8,128)(2,1)} %copy.11), kind=kOutput, calls=%fused_computation.10 | convolution fusion | flops 1073741824 | bytes 33554432 | tf_op jit(solution)/shard_map/sckbi,sckbj->bkij/dot_general | solution.py:61
  434.3 14.9 %convolution_bitcast_fusion = f32[16,1,16,128,128]{4,3,2,0,1:T(8,128)} fusion(bf16[64,2,16,16,128]{4,0,1,2,3:T(8,128)(2,1)} %copy.15, bf16[64,1,16,16,128]{4,0,1,2,3:T(8,128)(2,1)} %get-tuple-element.6, bf16[64,1,16,16,128]{4,0,1,2,3:T(8,128)(2,1)} %get-tuple-element.5), kind=kOutput, calls=%fused_computation.9 | convolution fusion | flops 1077936128 | bytes 33554432 | tf_op jit(solution)/shard_map/sckbi,sckbj->bkij/dot_general | solution.py:62
  449.2 12.2 %maximum_multiply_fusion = f32[16,2,16,128,128]{4,3,2,0,1:T(8,128)S(1)} fusion(f32[16,1,16,128,128]{4,3,2,0,1:T(8,128)} %convolution_bitcast_fusion, f32[16,1,16,128,128]{4,3,2,0,1:T(8,128)} %convolution_bitcast_fusion.1), kind=kLoop, calls=%fused_computation.3 | loop fusion | flops 16777216 | bytes 67108864 | tf_op jit(solution)/shard_map/div | solution.py:63
  461.4 0.0 copy-start.1
  461.4 11.3 %copy.17 = f32[16,2,16,128,128]{4,3,2,1,0:T(8,128)} copy(f32[16,2,16,128,128]{4,3,2,0,1:T(8,128)S(1)} %maximum_multiply_fusion) | data formatting | bytes 67108864 | tf_op jit(solution)/shard_map/div | solution.py:63
  472.7 0.0 copy-done.1
  (6 shorter events, 0.0 us)
Async XLA Ops:
  0.0 111.3 %copy-start = (s32[2048]{0:T(1024)S(1)}, s32[2048]{0:T(1024)}, u32[]{:S(2)}) copy-start(s32[2048]{0:T(1024)} %param.4) | copy-start | bytes 24580
  6.6 71.9 %collective-permute-start = (bf16[3,512,2048]{2,1,0:T(8,128)(2,1)}, bf16[3,512,2048]{2,1,0:T(8,128)(2,1)}, u32[]{:S(2)}, u32[]{:S(2)}) collective-permute-start(bf16[3,512,2048]{2,1,0:T(8,128)(2,1)} %bitcast), channel_id=1, source_target_pairs={{0,1},{1,2},{2,3},{3,4},{4,5},{5,6},{6,7},{7,8},{8,9},{9,10},{10,1... | collective-permute-start | bytes 18874376 | tf_op jit(solution)/shard_map/ppermute | solution.py:14
  95.6 15.5 %copy-start.2 = (s32[16,2]{0,1:T(2,128)S(1)}, s32[16,2]{0,1:T(2,128)}, u32[]{:S(2)}) copy-start(s32[16,2]{0,1:T(2,128)} %param.5) | copy-start | bytes 388
  103.9 189.6 %all-to-all-start = ((bf16[4,2,16,16,2048]{4,3,1,0,2:T(8,128)(2,1)}), bf16[4,2,16,16,2048]{4,3,1,0,2:T(8,128)(2,1)}, u32[]{:S(2)}, u32[]{:S(2)}) async-start(bf16[4,2,16,16,2048]{4,3,1,0,2:T(8,128)(2,1)} %copy.7), calls=%async_computation | async-start | bytes 16777216 | tf_op jit(solution)/shard_map/all_to_all | solution.py:56
  461.4 11.3 %copy-start.1 = (s32[2048]{0:T(1024)S(1)}, s32[2048]{0:T(1024)}, u32[]{:S(2)}) copy-start(s32[2048]{0:T(1024)} %param.4) | copy-start | bytes 24580
where the time goes:
time: 474 us; the launch traced here: 473 us
  waiting for transfers between devices  246 us (52%)
  local copies, waits for them, and re-layouts  148 us (31%)
  matrix products  46.3 us (10%)
  other arithmetic  20.9 us (4%)
  starting transfers between devices  10.9 us (2%)
    all_to_all x1, waiting for transfers between devices, body(): lax.all_to_all(spectra, 'tm', split_axis=2, concat_axis=0, tiled=True)  182 us
    ppermute x1, waiting for transfers between devices, from_behind(): return lax.ppermute(block, axis, route)  64.7 us
    gather x2, local copies, waits for them, and re-layouts, body(): second = data[:, :, :, columns[:, 1]]  47 us
    gather x2, local copies, waits for them, and re-layouts, body(): first = data[:, :, :, columns[:, 0]]  46.9 us
    squeeze x1, local copies, waits for them, and re-layouts, body(): lax.all_to_all(spectra, 'tm', split_axis=2, concat_axis=0, tiled=True)  26.8 us
    dot_general x1, matrix products, body(): jnp.einsum('kn,sni->ski', table, filtered, preferred_element_type=jnp.flo...  17.1 us
    dot_general x1, matrix products, body(): jnp.einsum('sckbi,sckbj->bkij', flipped, second, preferred_element_type=j...  14.9 us
    dot_general x1, matrix products, body(): jnp.einsum('sckbi,sckbj->bkij', first, second, preferred_element_type=jnp...  14.4 us
  transfers between devices with their start and end apart: 2, of which 2 were waited for; matrix products, arithmetic and copies ran while one was open for 1% of the time, Pallas kernels for 0%

commit v1 on v0

v1 whole, which is shorter than its diff:
```python
import functools

import jax
import jax.numpy as jnp
import ml_dtypes
import numpy as np
from jax import lax
from jax.experimental import pallas as pl
from jax.experimental.pallas import tpu as pltpu
from jax.sharding import PartitionSpec as P

CHANNELS = 256
TAPS = 4
PANEL = 128
USED = 8
WIDE = 256
MESH = pl.DeviceIdType.MESH


def filter_taps(taps, frame):
    length = taps * frame
    place = np.arange(length).astype(np.float64)
    middle = (length - 1) / 2.0
    window = 0.5 - 0.5 * np.cos(2.0 * np.pi * (place + 0.5) / length)
    shape_h = np.sinc((place - middle) / frame) * window
    shape_h = shape_h / np.sqrt(np.sum(shape_h * shape_h))
    return shape_h.reshape(taps, frame).astype(np.float32)


def dft_table(channels):
    frame = 2 * channels
    rows_k = np.arange(channels)[:, None]
    cols_n = np.arange(frame)[None, :]
    phase = (rows_k * cols_n % frame) * (2.0 * np.pi / frame)
    table = np.stack([np.cos(phase), -np.sin(phase)], axis=0)
    return table.astype(ml_dtypes.bfloat16).astype(np.float32)


def filterbank_matrix(spec_dev):
    frame = 2 * CHANNELS
    coeff = filter_taps(TAPS, frame)
    table = dft_table(CHANNELS)
    padded = spec_dev + TAPS - 1
    full = np.zeros((CHANNELS, spec_dev, 2, padded, frame), np.float32)
    for s in range(spec_dev):
        for t in range(TAPS):
            full[:, s, :, s + t, :] = np.moveaxis(table * coeff[t], 0, 1)
    return full.reshape(CHANNELS * spec_dev * 2, padded * frame).astype(ml_dtypes.bfloat16)


def regroup_matrix(sources, spec_dev):
    per = 2 * spec_dev
    pair = 16 // per
    out = np.zeros((pair, 2, sources, spec_dev, 2, sources, pair, spec_dev, 2), np.float32)
    for f in range(pair):
        for g in range(sources):
            for s in range(spec_dev):
                out[f, 0, g, s, 0, g, f, s, 0] = 1
                out[f, 0, g, s, 1, g, f, s, 1] = 1
                out[f, 1, g, s, 0, g, f, s, 1] = 1
                out[f, 1, g, s, 1, g, f, s, 0] = -1
    return out.reshape(pair, 2, sources * per, sources * 16).astype(ml_dtypes.bfloat16)


def exchange_kernel(n, chunks, volt_hbm, mat_hbm, cols_ref, data_ref, volt, mat, onehot,
                    padded, spectra, load_sem, halo_send, halo_recv, own_sem, send_sem, recv_sem):
    me = lax.axis_index("tm")
    rows, width = volt.shape
    head = padded.shape[1] - rows
    total = spectra.shape[1]
    block = total // n
    tile = 512
    load_v = pltpu.make_async_copy(volt_hbm, volt, load_sem.at[0])
    load_m = pltpu.make_async_copy(mat_hbm, mat, load_sem.at[1])
    load_v.start()
    load_m.start()
    barrier = pltpu.get_barrier_semaphore()

    def greet(k, carry):
        peer = lax.rem(me + k, n)
        pl.semaphore_signal(barrier, inc=1, device_id={"tm": peer}, device_id_type=MESH)
        return carry

    lax.fori_loop(1, n, greet, 0)

    def select(c):
        cols = cols_ref[:, c * WIDE : (c + 1) * WIDE]

        def mark(i, carry):
            at = pl.multiple_of(i * 256, 256)
            place = lax.broadcasted_iota(jnp.int32, (256, WIDE), 0) + at
            onehot[pl.ds(at, 256), :] = jnp.where(place == cols, 1.0, 0.0).astype(jnp.bfloat16)
            return carry

        lax.fori_loop(0, width // 256, mark, 0)
        if c == 0:
            load_v.wait()

        def pick(i, carry):
            at = pl.multiple_of(i * tile, tile)
            got = jnp.dot(volt[pl.ds(at, tile), :], onehot[...], preferred_element_type=jnp.float32)
            padded[c, pl.ds(pl.multiple_of(head + at, tile), tile), :] = got.astype(jnp.bfloat16)
            return carry

        lax.fori_loop(0, rows // tile, pick, 0)

    def halo(c):
        return pltpu.make_async_remote_copy(
            src_ref=padded.at[c, pl.ds(rows, head), :],
            dst_ref=padded.at[c, pl.ds(0, head), :],
            send_sem=halo_send.at[c],
            recv_sem=halo_recv.at[c],
            device_id={"tm": lax.rem(me + 1, n)},
            device_id_type=MESH,
        )

    def send_halo(c):
        @pl.when(me < n - 1)
        def _():
            halo(c).start()

    def piece(c, k):
        peer = lax.rem(me + k, n)
        return pltpu.make_async_remote_copy(
            src_ref=spectra.at[c, pl.ds(pl.multiple_of(peer * block, block), block), :],
            dst_ref=data_ref.at[c, me],
            send_sem=send_sem.at[c, k],
            recv_sem=recv_sem.at[c, k],
            device_id={"tm": peer},
            device_id_type=MESH,
        )

    def own(c):
        return pltpu.make_async_copy(
            spectra.at[c, pl.ds(pl.multiple_of(me * block, block), block), :],
            data_ref.at[c, me],
            own_sem.at[c],
        )

    def channelize(c):
        @pl.when(me > 0)
        def _():
            halo(c).wait_recv()

        @pl.when(me == 0)
        def _():
            padded[c, pl.ds(0, head), :] = jnp.zeros((head, WIDE), jnp.bfloat16)

        if c == 0:
            load_m.wait()

        def run(i, carry):
            at = pl.multiple_of(i * tile, tile)
            got = jnp.dot(mat[pl.ds(at, tile), :], padded[c], preferred_element_type=jnp.float32)
            spectra[c, pl.ds(at, tile), :] = got.astype(jnp.bfloat16)
            return carry

        lax.fori_loop(0, total // tile, run, 0)

    def send(c):
        def one(k, carry):
            piece(c, k).start()
            return carry

        lax.fori_loop(1, n, one, 0)
        own(c).start()

    ahead = min(2, chunks)
    for c in range(ahead):
        select(c)
        if c == 0:
            pl.semaphore_wait(barrier, n - 1)
        send_halo(c)
    for c in range(chunks):
        channelize(c)
        send(c)
        if c + ahead < chunks:
            select(c + ahead)
            send_halo(c + ahead)
    for c in range(chunks):
        @pl.when(me < n - 1)
        def _():
            halo(c).wait_send()

        own(c).wait()

        def finish(k, carry):
            piece(c, k).wait()
            return carry

        lax.fori_loop(1, n, finish, 0)


def exchange(voltages, matrix, cols, n):
    rows, width = voltages.shape
    total, depth = matrix.shape
    chunks = cols.shape[1] // WIDE
    block = total // n
    return pl.pallas_call(
        functools.partial(exchange_kernel, n, chunks),
        out_shape=jax.ShapeDtypeStruct((chunks, n, block, WIDE), jnp.bfloat16),
        in_specs=[
            pl.BlockSpec(memory_space=pl.ANY),
            pl.BlockSpec(memory_space=pl.ANY),
            pl.BlockSpec(memory_space=pltpu.VMEM),
        ],
        out_specs=pl.BlockSpec(memory_space=pl.ANY),
        scratch_shapes=[
            pltpu.VMEM((rows, width), jnp.bfloat16),
            pltpu.VMEM((total, depth), jnp.bfloat16),
            pltpu.VMEM((width, WIDE), jnp.bfloat16),
            pltpu.VMEM((chunks, depth, WIDE), jnp.bfloat16),
            pltpu.VMEM((chunks, total, WIDE), jnp.bfloat16),
            pltpu.SemaphoreType.DMA((2,)),
            pltpu.SemaphoreType.DMA((chunks,)),
            pltpu.SemaphoreType.DMA((chunks,)),
            pltpu.SemaphoreType.DMA((chunks,)),
            pltpu.SemaphoreType.DMA((chunks, n)),
            pltpu.SemaphoreType.DMA((chunks, n)),
        ],
        compiler_params=pltpu.CompilerParams(
            collective_id=0, has_side_effects=True, vmem_limit_bytes=56 * 1024 * 1024
        ),
        name="channelize_exchange",
    )(voltages, matrix, cols)


def correlate_kernel(scale, slots, data_ref, plain_ref, both_ref, out_ref, lhs, rhs):
    chunks, sources, group, _ = data_ref.shape
    pair = out_ref.shape[2]
    depth = rhs.shape[2]
    per = WIDE // PANEL
    for c in range(chunks):
        got = data_ref[c].reshape(sources * group, WIDE)
        second = jnp.dot(plain_ref[...], got, preferred_element_type=jnp.float32)
        second = second.astype(jnp.bfloat16)
        first = lax.dot_general(
            got, both_ref[...], (((0,), (1,)), ((), ())), preferred_element_type=jnp.float32
        )
        first = (first * scale).astype(jnp.bfloat16)
        for h in range(per):
            for f in range(pair):
                rhs[c * per + h, f] = second[
                    f * depth : (f + 1) * depth, h * PANEL : (h + 1) * PANEL
                ]
                for kind in range(2):
                    at = (f * 2 + kind) * depth
                    lhs[c * per + h, f, kind * PANEL : (kind + 1) * PANEL, :] = first[
                        h * PANEL : (h + 1) * PANEL, at : at + depth
                    ]

    for b in range(out_ref.shape[0]):
        a, w = slots[2 * b], slots[2 * b + 1]
        for f in range(pair):
            got = jnp.dot(lhs[a, f], rhs[w, f], preferred_element_type=jnp.float32)
            out_ref[b, 0, f] = got[:PANEL]
            out_ref[b, 1, f] = got[PANEL:]


def correlate(data, slots, spec_dev, band_dev):
    chunks, sources, block, _ = data.shape
    pair = 16 // (2 * spec_dev)
    depth = sources * spec_dev * 2
    blocks = slots.shape[0] // 2
    regroup = regroup_matrix(sources, spec_dev)
    plain = jnp.asarray(regroup[:, 0].reshape(pair * depth, sources * 16))
    both = jnp.asarray(regroup.reshape(pair * 2 * depth, sources * 16))
    return pl.pallas_call(
        functools.partial(correlate_kernel, 1.0 / (sources * spec_dev)),
        out_shape=jax.ShapeDtypeStruct((blocks, 2, band_dev, PANEL, PANEL), jnp.float32),
        grid_spec=pltpu.PrefetchScalarGridSpec(
            num_scalar_prefetch=1,
            grid=(band_dev // pair,),
            in_specs=[
                pl.BlockSpec((chunks, sources, 16, WIDE), lambda j, s: (0, 0, j, 0)),
                pl.BlockSpec(plain.shape, lambda j, s: (0, 0)),
                pl.BlockSpec(both.shape, lambda j, s: (0, 0)),
            ],
            out_specs=pl.BlockSpec((blocks, 2, pair, PANEL, PANEL), lambda j, s: (0, 0, j, 0, 0)),
            scratch_shapes=[
                pltpu.VMEM((USED, pair, 2 * PANEL, depth), jnp.bfloat16),
                pltpu.VMEM((USED, pair, depth, PANEL), jnp.bfloat16),
            ],
        ),
        compiler_params=pltpu.CompilerParams(vmem_limit_bytes=48 * 1024 * 1024),
        name="correlate",
    )(slots, data, plain, both)


def body(voltages, panel_map, block_list):
    frame = 2 * CHANNELS
    spec_dev = voltages.shape[0] // frame
    groups = lax.axis_size("tm")
    band_dev = CHANNELS // groups
    panels = panel_map.shape[0] // PANEL
    named = jnp.any(block_list.reshape(-1)[:, None] == jnp.arange(panels)[None, :], axis=0)
    before = jnp.arange(panels)[None, :] < jnp.arange(panels)[:, None]
    rank = jnp.sum(jnp.where(before & named[None, :], 1, 0), axis=1)
    at_slot = named[None, :] & (rank[None, :] == jnp.arange(USED)[:, None])
    panel_rows = panel_map.reshape(panels, PANEL)
    cols = jnp.sum(jnp.where(at_slot[:, :, None], panel_rows[None], 0), axis=1)
    flat = block_list.reshape(-1)
    slots = jnp.sum(jnp.where(flat[:, None] == jnp.arange(panels)[None, :], rank[None, :], 0), axis=1)
    matrix = jnp.asarray(filterbank_matrix(spec_dev))
    data = exchange(voltages, matrix, cols.reshape(1, USED * PANEL).astype(jnp.int32), groups)
    return correlate(data, slots.astype(jnp.int32), spec_dev, band_dev)


def solution(mesh):
    in_specs = (P(("band", "tm"), None), P(), P())
    out_specs = P("band", None, "tm", None, None)
    return jax.shard_map(body, mesh=mesh, in_specs=in_specs, out_specs=out_specs, check_vma=False)
```

time: 474 us -> 159 us (0.34)
  waiting for transfers between devices: 246 us -> 0 us
  Pallas kernels: 0 us -> 153 us
  local copies, waits for them, and re-layouts: 148 us -> 3.08 us
  matrix products: 46.3 us -> 0 us
  other arithmetic: 20.9 us -> 1.72 us
  starting transfers between devices: 10.9 us -> 0 us
    all_to_all x1 -> x0, waiting for transfers between devices: 182 us -> none  [body(): lax.all_to_all(spectra, 'tm', split_axis=2, concat_axis=0, tiled=True)]
    pallas_call x0 -> x2, Pallas kernels: none -> 153 us  [the longest x1 138 us: exchange(): pl.pallas_call(functools.partial(exchange_kernel, n, chunks), out_shape=j...]
    gather x5 -> x0, local copies, waits for them, and re-layouts: 94.4 us -> none  [the longest x2 47 us: body(): second = data[:, :, :, columns[:, 1]]]
    ppermute x1 -> x0, waiting for transfers between devices: 64.7 us -> none  [from_behind(): return lax.ppermute(block, axis, route)]
    dot_general x3 -> x0, matrix products: 46.3 us -> none  [the longest x1 17.1 us: body(): jnp.einsum('kn,sni->ski', table, filtered, preferred_element_type=jnp.flo...]
    squeeze x1 -> x0, local copies, waits for them, and re-layouts: 26.8 us -> none  [body(): lax.all_to_all(spectra, 'tm', split_axis=2, concat_axis=0, tiled=True)]
    div x2 -> x0, other arithmetic: 12.2 us -> none  [the longest x1 12.2 us: body(): return jnp.stack([real_part, imag_part], axis=1) / total]
    div x1 -> x0, local copies, waits for them, and re-layouts: 11.3 us -> none  [body(): return jnp.stack([real_part, imag_part], axis=1) / total]
  transfers between devices with their start and end apart: 2 -> 0, of which waited for: 2 -> 0; matrix products, arithmetic and copies ran while one was open for 1% -> 0% of each run, Pallas kernels for 0% -> 0%
where the time goes in v1:
time: 159 us; the launch traced here: 158 us
  Pallas kernels  153 us (96%)
  local copies, waits for them, and re-layouts  3.08 us (2%)
  other arithmetic  1.72 us (1%)
    pallas_call x1, Pallas kernels, exchange(): pl.pallas_call(functools.partial(exchange_kernel, n, chunks), out_shape=j...  138 us
    pallas_call x1, Pallas kernels, correlate(): pl.pallas_call(functools.partial(correlate_kernel, 1.0 / (sources * spec_...  15.4 us

profile of v1, /device:TPU:13, one launch (start us, length us, event | category | flops | bytes accessed | tf_op | source)
XLA Modules:
  0.0 158.0 jit_solution(17004468092020682302)
XLA Ops:
  0.0 0.0 copy-start.1
  0.0 0.0 copy-start.2
  0.0 0.8 copy.9
  0.8 0.1 eq.18
  0.9 0.1 fusion
  1.0 0.1 select_reduce_fusion.2
  1.1 0.1 select_reduce_fusion.1.slots
  1.2 1.4 select_reduce_fusion
  2.6 137.8 %channelize_exchange.1.data_ref = bf16[4,16,128,256]{3,2,1,0:T(8,128)(2,1)} custom-call(bf16[2048,2048]{1,0:T(8,128)(2,1)} %volt_hbm.1, bf16[2048,3584]{1,0:T(8,128)(2,1)} %constant.12.clone.mat_hbm, s32[1,1024]{1,0:T(1,128)} %bitcast.2), custom_call_target="tpu_custom_call" | custom-call | tf_op jit(solution)/shard_map/channelize_exchange/pallas_call | solution.py:199
  140.4 0.0 copy-done.1
  140.5 0.0 copy-done.2
  140.5 0.0 copy-start
  140.5 2.2 %copy-done = bf16[4,16,128,256]{3,2,1,0:T(8,128)(2,1)S(1)} copy-done((bf16[4,16,128,256]{3,2,1,0:T(8,128)(2,1)S(1)}, bf16[4,16,128,256]{3,2,1,0:T(8,128)(2,1)}, u32[]{:S(2)}) %copy-start) | copy-done | bytes 4194328
  142.7 15.4 %correlate.1 = f32[16,2,16,128,128]{4,3,2,1,0:T(8,128)} custom-call(s32[32]{0:T(128)S(1)} %select_reduce_fusion.1.slots, bf16[4,16,128,256]{3,2,1,0:T(8,128)(2,1)S(1)} %copy-done, bf16[256,256]{1,0:T(8,128)(2,1)S(1)} %copy-done.2, bf16[512,256]{1,0:T(8,128)(2,1)S(1)} %copy-done.1), custom_call_target="tpu_custom_call" | custom-call | tf_op jit(solution)/shard_map/correlate/pallas_call | solution.py:268
  (1 shorter events, 0.0 us)
Async XLA Ops:
  0.0 140.4 %copy-start.1 = (bf16[512,256]{1,0:T(8,128)(2,1)S(1)}, bf16[512,256]{1,0:T(8,128)(2,1)}, u32[]{:S(2)}) copy-start(bf16[512,256]{1,0:T(8,128)(2,1)} %constant.14.clone.both_ref) | copy-start | bytes 786436
  0.0 140.5 %copy-start.2 = (bf16[256,256]{1,0:T(8,128)(2,1)S(1)}, bf16[256,256]{1,0:T(8,128)(2,1)}, u32[]{:S(2)}) copy-start(bf16[256,256]{1,0:T(8,128)(2,1)} %constant.13.clone.plain_ref) | copy-start | bytes 393220
  140.5 2.2 %copy-start = (bf16[4,16,128,256]{3,2,1,0:T(8,128)(2,1)S(1)}, bf16[4,16,128,256]{3,2,1,0:T(8,128)(2,1)}, u32[]{:S(2)}) copy-start(bf16[4,16,128,256]{3,2,1,0:T(8,128)(2,1)} %channelize_exchange.1.data_ref) | copy-start | bytes 12582916
